TPU v7x, 128 devices: a whole 4x4x4 slice. The times are simulated.
128 devices in a mesh: pb: 16 (over z_hi, y, core), ka: 8 (over z_lo, x).
Axes of the slice: x: 4, y: 4, z: 4 (z_hi: 2, z_lo: 2; z = z_hi * 2 + z_lo), core: 2. Of those that a mesh axis runs over, the one named last changes fastest.
Arguments:
- queries: bfloat16 [16384, 4096], P('pb'), may hold values from -6 to 6
- key_rows: bfloat16 [16384, 512], P(('pb', 'ka')), may hold values from -6 to 6
- values: bfloat16 [16384, 512], P(('pb', 'ka')), may hold values from -6 to 6
- attn_out: bfloat16 [16384, 4096], P(('pb', 'ka')), may hold values from -6 to 6
- grad_out: bfloat16 [16384, 4096], P('pb'), may hold values from -6 to 6
- log_sums: float32 [32, 16384], P(None, ('pb', 'ka')), may hold values from 3 to 7
- key_gain: float32 [512], replicated, may hold values from 0.25 to 1.75
- value_gain: float32 [512], replicated, may hold values from 0.25 to 1.75
- doc_ids: int32 [128], replicated, may hold values from 0 to 15, never falling along the last dimension, each value on 1 to 64 neighbouring positions
- tile_mask: int32 [128, 128], replicated, may hold values 0 or 1
- block_order: int32 [128], replicated, may hold values from 0 to 127, each once
Outputs:
- grad_queries: bfloat16 [16384, 4096], P(('pb', 'ka'))
- grad_keys: bfloat16 [16384, 512], P(('pb', 'ka'))
- grad_values: bfloat16 [16384, 512], P(('pb', 'ka'))
- grad_key_gain: float32 [512], replicated
- grad_value_gain: float32 [512], replicated
Inputs may be any that keep to these rules, and one draw needn't show every extreme that they name: `doc_ids`: documents are numbered in sequence order; each spans 1 to 64 tiles, one exactly that many. `block_order`: each sequence tile once.
All inputs are finite; a program needn't handle non-finite values.
Results may differ from a plain program's by a relative error of at most 0.015.
Values may be sent and summed in bfloat16 or wider, within the bound.
A program may use at most 192 MiB of HBM per device.

v0:
```python
import jax
import jax.numpy as jnp
from jax import lax
from jax.sharding import PartitionSpec as P

HEAD_DIM = 128
TILE = 128


def add_rows(total, start, term):
    current = lax.dynamic_slice_in_dim(total, start, term.shape[0], 0)
    return lax.dynamic_update_slice_in_dim(total, current + term, start, 0)


def select_by(source, picks):
    ranks = jnp.arange(source.shape[0], dtype=jnp.int32)
    return jnp.sum(jnp.where(picks[:, None] == ranks[None, :], source[None, :], 0), axis=1)


def shards(
    queries,
    key_rows,
    values,
    attn_out,
    grad_out,
    log_sums,
    key_gain,
    value_gain,
    doc_ids,
    tile_mask,
    block_order,
):
    count_pb = lax.axis_size("pb")
    count_ka = lax.axis_size("ka")
    place_pb = lax.axis_index("pb")
    place_ka = lax.axis_index("ka")
    rows_dev = key_rows.shape[0]
    query_rows = queries.shape[0]
    head_count = log_sums.shape[0]
    kv_width = key_rows.shape[1]
    kv_heads = kv_width // HEAD_DIM
    group_size = head_count // kv_heads
    feat_width = head_count * HEAD_DIM
    score_scale = HEAD_DIM ** (-0.5)
    tiles_dev = rows_dev // TILE
    query_tiles = query_rows // TILE
    key_tiles = count_pb * tiles_dev
    tile_total = block_order.shape[0]
    own_grad = lax.dynamic_slice_in_dim(grad_out, place_ka * rows_dev, rows_dev, 0)
    products = own_grad.astype(jnp.float32) * attn_out.astype(jnp.float32)
    delta_own = jnp.sum(products.reshape(rows_dev, head_count, HEAD_DIM), axis=2).T
    lse_rows, delta_rows = (
        lax.all_gather(log_sums, "ka", axis=1, tiled=True),
        lax.all_gather(delta_own, "ka", axis=1, tiled=True),
    )
    key_all, value_all = (
        lax.all_gather(key_rows, "pb", axis=0, tiled=True),
        lax.all_gather(values, "pb", axis=0, tiled=True),
    )
    key_scaled = (key_all.astype(jnp.float32) * key_gain).astype(jnp.bfloat16)
    value_scaled = (value_all.astype(jnp.float32) * value_gain).astype(jnp.bfloat16)
    query_stored = place_pb * query_tiles + jnp.arange(query_tiles, dtype=jnp.int32)
    key_number = jnp.arange(key_tiles, dtype=jnp.int32)
    key_stored = (
        key_number // tiles_dev * count_ka + place_ka
    ) * tiles_dev + key_number % tiles_dev
    query_seq = select_by(block_order, query_stored)
    key_seq = select_by(block_order, key_stored)
    ranks = jnp.arange(tile_total, dtype=jnp.int32)
    mask_rows = jnp.sum(
        jnp.where((query_seq[:, None] == ranks[None, :])[:, :, None], tile_mask[None, :, :], 0),
        axis=1,
    )
    mask_pair = jnp.sum(
        jnp.where((key_seq[None, :] == ranks[:, None])[None, :, :], mask_rows[:, :, None], 0),
        axis=1,
    )
    doc_query = select_by(doc_ids, query_seq)
    doc_key = select_by(doc_ids, key_seq)
    active = (
        (mask_pair == 1)
        & (doc_query[:, None] == doc_key[None, :])
        & (query_seq[:, None] >= key_seq[None, :])
    )
    flat_live = active.reshape(-1).astype(jnp.int32)
    live_count = jnp.sum(flat_live)
    pair_order = jnp.argsort(1 - flat_live, stable=True)
    offsets = jnp.arange(TILE, dtype=jnp.int32)
    loop_start = jnp.int32(0)

    def tile_grads(step_at):
        pair_at = pair_order[step_at]
        query_at = pair_at // key_tiles
        key_at = pair_at % key_tiles
        query_tile = lax.dynamic_slice_in_dim(queries, query_at * TILE, TILE, 0).reshape(
            TILE, kv_heads, group_size, HEAD_DIM
        )
        grad_tile = lax.dynamic_slice_in_dim(grad_out, query_at * TILE, TILE, 0).reshape(
            TILE, kv_heads, group_size, HEAD_DIM
        )
        key_tile = lax.dynamic_slice_in_dim(key_scaled, key_at * TILE, TILE, 0).reshape(
            TILE, kv_heads, HEAD_DIM
        )
        value_tile = lax.dynamic_slice_in_dim(value_scaled, key_at * TILE, TILE, 0).reshape(
            TILE, kv_heads, HEAD_DIM
        )
        lse_tile = lax.dynamic_slice_in_dim(lse_rows, query_at * TILE, TILE, 1).reshape(
            kv_heads, group_size, TILE
        )
        delta_tile = lax.dynamic_slice_in_dim(delta_rows, query_at * TILE, TILE, 1).reshape(
            kv_heads, group_size, TILE
        )
        query_pos = lax.dynamic_index_in_dim(query_seq, query_at, keepdims=False) * TILE + offsets
        key_pos = lax.dynamic_index_in_dim(key_seq, key_at, keepdims=False) * TILE + offsets
        allowed = query_pos[:, None] >= key_pos[None, :]
        scores = (
            jnp.einsum("ihgd,jhd->hgij", query_tile, key_tile, preferred_element_type=jnp.float32)
            * score_scale
        )
        weights = jnp.where(allowed, jnp.exp(scores - lse_tile[..., None]), 0.0)
        dweights = jnp.einsum(
            "ihgd,jhd->hgij", grad_tile, value_tile, preferred_element_type=jnp.float32
        )
        dscores = (weights * (dweights - delta_tile[..., None])).astype(jnp.bfloat16)
        query_term = None
        key_term = None
        value_term = None
        weights_low = weights.astype(jnp.bfloat16)
        value_term = jnp.einsum(
            "hgij,ihgd->jhd", weights_low, grad_tile, preferred_element_type=jnp.float32
        ).reshape(TILE, kv_width)
        key_term = (
            jnp.einsum("hgij,ihgd->jhd", dscores, query_tile, preferred_element_type=jnp.float32)
            * score_scale
        ).reshape(TILE, kv_width)
        query_term = (
            jnp.einsum("hgij,jhd->ihgd", dscores, key_tile, preferred_element_type=jnp.float32)
            * score_scale
        ).reshape(TILE, feat_width)
        return (query_at * TILE, key_at * TILE, query_term, key_term, value_term)

    def joint_step(step_at, totals):
        query_sum, key_sum, value_sum = totals
        query_start, key_start, query_term, key_term, value_term = tile_grads(step_at)
        return (
            add_rows(query_sum, query_start, query_term),
            add_rows(key_sum, key_start, key_term),
            add_rows(value_sum, key_start, value_term),
        )

    empty_query = jnp.zeros((query_rows, feat_width), jnp.float32)
    empty_key = jnp.zeros((key_all.shape[0], kv_width), jnp.float32)
    query_sum, key_sum, value_sum = lax.fori_loop(
        loop_start, live_count, joint_step, (empty_query, empty_key, empty_key)
    )
    key_mine = lax.psum_scatter(key_sum, "pb", scatter_dimension=0, tiled=True)
    value_mine = lax.psum_scatter(value_sum, "pb", scatter_dimension=0, tiled=True)
    gains = lax.psum(
        (
            jnp.sum(key_mine * key_rows.astype(jnp.float32), axis=0),
            jnp.sum(value_mine * values.astype(jnp.float32), axis=0),
        ),
        ("pb", "ka"),
    )
    key_mine, value_mine, gains = (key_mine, value_mine, gains)
    query_mine = lax.psum_scatter(
        query_sum.astype(jnp.bfloat16), "ka", scatter_dimension=0, tiled=True
    )
    grad_keys = (key_mine * key_gain).astype(jnp.bfloat16)
    grad_values = (value_mine * value_gain).astype(jnp.bfloat16)
    return (query_mine, grad_keys, grad_values, gains[0], gains[1])


def solution(mesh):
    placed = (
        P("pb", None),
        P(("pb", "ka"), None),
        P(("pb", "ka"), None),
        P(("pb", "ka"), None),
        P("pb", None),
        P(None, ("pb", "ka")),
        P(),
        P(),
        P(),
        P(),
        P(),
    )
    return jax.shard_map(
        shards,
        mesh=mesh,
        in_specs=placed,
        out_specs=(P(("pb", "ka"), None), P(("pb", "ka"), None), P(("pb", "ka"), None), P(), P()),
        check_vma=False,
    )
```

profile of v0, /device:TPU:1, one launch (start us, length us, event | category | flops | bytes accessed | tf_op | source)
XLA Modules:
  0.0 1504.9 jit_solution(9003434308373366913)
XLA Ops:
  18.5 24.2 %all_gather.15 = f32[32,1024]{0,1:T(8,128)S(1)} all-gather(f32[32,128]{0,1:T(8,128)S(1)} %bitcast.121), channel_id=1, replica_groups=mesh['pb'=16,'ka'=8] {'ka'}, dimensions={1}, use_global_device_ids=true | all-gather | bytes 147456 | tf_op jit(solution)/shard_map/all_gather | solution.py:54
  42.9 2.5 sort.17
  45.4 22.7 %all_gather.13 = f32[32,1024]{1,0:T(8,128)S(1)} all-gather(f32[32,128]{1,0:T(8,128)S(1)} %copy-done.11), channel_id=1, replica_groups=mesh['pb'=16,'ka'=8] {'ka'}, dimensions={1}, use_global_device_ids=true | all-gather | bytes 147456 | tf_op jit(solution)/shard_map/all_gather | solution.py:53
  68.8 2.0 multiply_convert_fusion.1
  70.8 45.0 %all-gather.5.cloned.1.call-done = bf16[2048,512]{0,1:T(8,128)(2,1)} async-done(((bf16[128,512]{0,1:T(8,128)(2,1)}), bf16[2048,512]{0,1:T(8,128)(2,1)}) %all-gather.5.cloned.1.call-update) | async-done | bytes 2097168 | tf_op jit(solution)/shard_map/all_gather | solution.py:58
  115.8 3.3 multiply_convert_fusion
  119.1 2.5 broadcast_in_dim.127.clone2
  121.6 2.5 broadcast_in_dim.127.clone
  124.1 7.8 broadcast_in_dim.126.clone
  131.9 305.1 %while.18 = (s32[]{:T(128)}, f32[1024,4096]{1,0:T(8,128)}, f32[2048,512]{1,0:T(8,128)}, f32[2048,512]{1,0:T(8,128)}, s32[]{:T(128)}, /*index=5*/s32[128]{0:T(128...) while((s32[]{:T(128)}, f32[1024,4096]{1,0:T(8,128)}, ...), condition=%wide.region_10.11_spmd.clone.clone, body=%wide.region_9.10_spmd.clone.clone.sunk | while | flops 676020480 | bytes 75046792 | solution.py:153
  159.1 3.3 constant_dynamic-update-slice_fusion.6
  189.6 3.3 constant_dynamic-update-slice_fusion.6
  220.0 3.2 constant_dynamic-update-slice_fusion.6
  250.5 3.2 constant_dynamic-update-slice_fusion.6
  280.9 3.2 constant_dynamic-update-slice_fusion.6
  311.4 3.2 constant_dynamic-update-slice_fusion.6
  341.8 3.2 constant_dynamic-update-slice_fusion.6
  372.2 3.2 constant_dynamic-update-slice_fusion.6
  402.7 3.3 constant_dynamic-update-slice_fusion.6
  433.1 3.3 constant_dynamic-update-slice_fusion.6
  437.7 9.0 convert_element_type.63
  446.8 828.1 %reduce-scatter.8.cloned.1.call-done = f32[128,512]{1,0:T(8,128)} async-done(((f32[2048,512]{1,0:T(8,128)}), f32[128,512]{1,0:T(8,128)}) %reduce-scatter.8.cloned.1.call-update) | async-done | bytes 262160 | tf_op jit(solution)/shard_map/reduce_scatter | solution.py:157
  1276.5 81.8 %reduce-scatter.6.cloned.1.call-done = f32[128,512]{1,0:T(8,128)} async-done(((f32[2048,512]{1,0:T(8,128)}), f32[128,512]{1,0:T(8,128)}) %reduce-scatter.6.cloned.1.call-update) | async-done | bytes 262160 | tf_op jit(solution)/shard_map/reduce_scatter | solution.py:156
  1360.0 138.5 %all-reduce = (f32[512]{0:T(512)}, f32[512]{0:T(512)}) all-reduce(f32[512]{0:T(512)S(1)} %get-tuple-element.358, f32[512]{0:T(512)S(1)} %get-tuple-element.356), channel_id=1, replica_groups=mesh['pb'=16,'ka'=8] {'pb','ka'}, use_global_device_ids=true, to_apply=%region_15.16 | all-reduce | flops 1024 | bytes 8192 | tf_op jit(solution)/shard_map/psum | solution.py:158
  (628 shorter events, 239.1 us)
Async XLA Ops:
  7.2 61.6 %all-gather.3.cloned.1.call-start = ((), (), s32[]{:S(2)}) async-start(), calls=%async_computation.3 | async-start | bytes 2228224 | tf_op jit(solution)/shard_map/all_gather | solution.py:57
  8.9 106.9 %all-gather.5.cloned.1.call-start = ((), (), s32[]{:S(2)}) async-start(), calls=%async_computation.4 | async-start | bytes 2228224 | tf_op jit(solution)/shard_map/all_gather | solution.py:58
  10.6 1264.2 %reduce-scatter.8.cloned.1.call-start = ((), (), s32[]{:S(2)}) async-start(), calls=%async_computation.7 | async-start | bytes 4456448 | tf_op jit(solution)/shard_map/reduce_scatter | solution.py:157
  17.8 27.6 %copy-start.11 = (f32[32,128]{1,0:T(8,128)S(1)}, f32[32,128]{1,0:T(8,128)}, u32[]{:S(2)}) copy-start(f32[32,128]{1,0:T(8,128)} %param.18) | copy-start | bytes 49156
  17.9 50.9 %copy-start.14 = (f32[512]{0:T(512)S(1)}, f32[512]{0:T(512)}, u32[]{:S(2)}) copy-start(f32[512]{0:T(512)} %param.19) | copy-start | bytes 6148
  68.8 47.0 %copy-start.12 = (f32[512]{0:T(512)S(1)}, f32[512]{0:T(512)}, u32[]{:S(2)}) copy-start(f32[512]{0:T(512)} %param.20) | copy-start | bytes 6148
  132.6 10.1 copy-start.7
  163.1 10.1 copy-start.7
  193.6 10.1 copy-start.7
  224.0 10.1 copy-start.7
  224.0 10.1 copy-start.16
  254.4 10.1 copy-start.7
  254.4 10.1 copy-start.16
  284.9 10.1 copy-start.7
  315.3 10.1 copy-start.7
  345.7 10.1 copy-start.7
  376.2 10.1 copy-start.7
  406.7 10.1 copy-start.7
  437.1 921.2 %reduce-scatter.6.cloned.1.call-start = ((), (), s32[]{:S(2)}) async-start(), calls=%async_computation.6 | async-start | bytes 4456448 | tf_op jit(solution)/shard_map/reduce_scatter | solution.py:156
  437.7 1060.7 %reduce-scatter.4.cloned.1.call-start = ((), (), s32[]{:S(2)}) async-start(), calls=%async_computation.5 | async-start | bytes 9437184 | tf_op jit(solution)/shard_map/reduce_scatter | solution.py:166
  446.8 828.1 %copy-start.5 = (bf16[128,512]{1,0:T(8,128)(2,1)S(1)}, bf16[128,512]{1,0:T(8,128)(2,1)}, u32[]{:S(2)}) copy-start(bf16[128,512]{1,0:T(8,128)(2,1)} %param.15) | copy-start | bytes 393220
  446.8 828.1 %copy-start.13 = (f32[512]{0:T(512)S(1)}, f32[512]{0:T(512)}, u32[]{:S(2)}) copy-start(f32[512]{0:T(512)} %param.20) | copy-start | bytes 6148
  446.8 911.6 %copy-start.6 = (bf16[128,512]{1,0:T(8,128)(2,1)S(1)}, bf16[128,512]{1,0:T(8,128)(2,1)}, u32[]{:S(2)}) copy-start(bf16[128,512]{1,0:T(8,128)(2,1)} %param.14) | copy-start | bytes 393220
  446.8 911.6 %copy-start.15 = (f32[512]{0:T(512)S(1)}, f32[512]{0:T(512)}, u32[]{:S(2)}) copy-start(f32[512]{0:T(512)} %param.19) | copy-start | bytes 6148
  (138 other events, 657.6 us)
Sparse Core Ops, SparseCore 0:
  10.8 54.0 all-gather.2
  67.8 47.9 all-gather.4
  437.2 837.6 reduce-scatter.7
  1279.3 78.9 reduce-scatter.5
  1361.1 93.0 reduce-scatter.3
where the time goes:
time: 1520 us; the launch traced here: 1500 us
  waiting for transfers between devices  955 us (63%)
  local copies, waits for them, and re-layouts  222 us (15%)
  blocking collectives  185 us (12%)
  loops' own time  49.4 us (3%)
  other arithmetic  47.6 us (3%)
  matrix products  31.2 us (2%)
    reduce_scatter x1, waiting for transfers between devices, shards(): lax.psum_scatter(value_sum, 'pb', scatter_dimension=0, tiled=True)  828 us
    psum x1, blocking collectives, shards(): lax.psum((jnp.sum(key_mine * key_rows.astype(jnp.float32), axis=0), jnp.s...  138 us
    reduce_scatter x1, waiting for transfers between devices, shards(): key_mine = lax.psum_scatter(key_sum, 'pb', scatter_dimension=0, tiled=True)  81.8 us
    dynamic_update_slice x60, local copies, waits for them, and re-layouts, add_rows(): return lax.dynamic_update_slice_in_dim(total, current + term, start, 0)  67.9 us
    dynamic_slice x50, local copies, waits for them, and re-layouts, add_rows(): current = lax.dynamic_slice_in_dim(total, start, term.shape[0], 0)  56.2 us
    another operation x1, loops' own time, shards(): lax.fori_loop(loop_start, live_count, joint_step, (empty_query, empty_key...  49.4 us
    all_gather x1, waiting for transfers between devices, shards(): lax.all_gather(values, 'pb', axis=0, tiled=True)  45 us
  transfers between devices with their start and end apart: 5, of which 3 were waited for; matrix products, arithmetic and copies ran while one was open for 2% of the time, Pallas kernels for 0%

commit v1 on v0

v1 whole, which is shorter than its diff:
```python
import functools
import math

import jax
import jax.numpy as jnp
from jax import lax
from jax.experimental import pallas as pl
from jax.experimental.pallas import tpu as pltpu
from jax.sharding import PartitionSpec as P


D = 128
T = 128
RING = 4
KA = 8
HEADS = 4
WIDTH = HEADS * D
QUERY_TILES = 16
KEY_TILES = 64
LOG2E = math.log2(math.e)
MESH = pl.DeviceIdType.MESH
F32 = jnp.float32
BF16 = jnp.bfloat16
NT = (((1,), (1,)), ((), ()))
TN = (((0,), (0,)), ((), ()))


def wrap(at):
    return lax.rem(at + RING, RING)


def place():
    pb, ka = lax.axis_index("pb"), lax.axis_index("ka")
    z = lax.div(pb, 8) * 2 + lax.div(ka, 4)
    return z, lax.rem(lax.div(pb, 2), 4), lax.rem(ka, 4), lax.rem(pb, 2)


def ident(z, y, x, c):
    return (lax.div(z, 2) * 8 + y * 2 + c, lax.rem(z, 2) * 4 + x)


def group_peers(z, y, x, c):
    ka = lax.rem(z, 2) * 4 + x
    peers = []
    for flip in range(2):
        for step in range(KA):
            if flip or step:
                to = lax.rem(ka + step, KA)
                core = 1 - c if flip else c
                peers.append((flip, step, ident(lax.div(z, 2) * 2 + lax.div(to, 4), y, lax.rem(to, 4), core)))
    return peers


def greet(devices):
    barrier = pltpu.get_barrier_semaphore()
    for device in devices:
        pl.semaphore_signal(barrier, inc=1, device_id=device, device_id_type=MESH)
    pl.semaphore_wait(barrier, len(devices))


class Lane:
    def __init__(self, sends, recvs, base):
        self.sends, self.recvs, self.base, self.out = sends, recvs, base, []

    def send(self, source, target, number, device):
        copy = pltpu.make_async_remote_copy(
            src_ref=source,
            dst_ref=target,
            send_sem=self.sends.at[self.base + number],
            recv_sem=self.recvs.at[self.base + number],
            device_id=device,
            device_id_type=MESH,
        )
        copy.start()
        self.out.append(copy)

    def arrive(self, target, number, device):
        pltpu.make_async_remote_copy(
            src_ref=target,
            dst_ref=target,
            send_sem=self.sends.at[self.base + number],
            recv_sem=self.recvs.at[self.base + number],
            device_id=device,
            device_id_type=MESH,
        ).wait_recv()

    def drain(self):
        for copy in self.out:
            copy.wait_send()
        self.out = []


class Spread(Lane):
    def setup(self, item, plus, minus):
        self.item, self.plus, self.minus = item, plus, minus
        half = item(0).shape[0] // 2
        self.first, self.second = pl.ds(0, half), pl.ds(half, half)
        return self

    def start(self):
        self.send(self.item(0), self.item(0), 0, self.plus)
        self.send(self.item(0), self.item(0), 1, self.minus)

    def relay_up(self):
        block = self.item(-1)
        self.arrive(block, 0, self.minus)
        self.send(block.at[self.first], block.at[self.first], 2, self.plus)

    def relay_down(self):
        block = self.item(1)
        self.arrive(block, 1, self.plus)
        self.send(block.at[self.second], block.at[self.second], 3, self.minus)

    def finish(self):
        block = self.item(2)
        self.arrive(block.at[self.first], 2, self.minus)
        self.arrive(block.at[self.second], 3, self.plus)


class Fold(Lane):
    def setup(self, half_of, put, land, plus, minus):
        self.half_of, self.put, self.land, self.plus, self.minus = half_of, put, land, plus, minus
        return self

    def start(self):
        self.send(self.half_of(2, 0), self.land.at[0], 0, self.plus)
        self.send(self.half_of(2, 1), self.land.at[1], 1, self.minus)
        self.send(self.half_of(1, 1), self.land.at[3], 3, self.plus)
        self.send(self.half_of(-1, 0), self.land.at[4], 4, self.minus)

    def relay(self):
        self.arrive(self.land.at[0], 0, self.minus)
        add_into(self.half_of(1, 0), [self.land.at[0]])
        self.send(self.half_of(1, 0), self.land.at[2], 2, self.plus)
        self.arrive(self.land.at[1], 1, self.plus)
        add_into(self.half_of(-1, 1), [self.land.at[1]])
        self.send(self.half_of(-1, 1), self.land.at[5], 5, self.minus)

    def finish(self):
        self.arrive(self.land.at[3], 3, self.minus)
        self.arrive(self.land.at[4], 4, self.plus)
        self.arrive(self.land.at[2], 2, self.minus)
        add_into(self.half_of(0, 0), [self.land.at[2], self.land.at[4]])
        self.arrive(self.land.at[5], 5, self.plus)
        add_into(self.half_of(0, 1), [self.land.at[3], self.land.at[5]])


def add_into(total, terms):
    rows = 256

    @pl.loop(0, total.shape[0] // rows)
    def _(n):
        at = pl.ds(pl.multiple_of(n * rows, rows), rows)
        value = total[at, :].astype(F32)
        for term in terms:
            value = value + term[at, :].astype(F32)
        total[at, :] = value.astype(total.dtype)


def head_columns(z, x):
    return pl.ds(pl.multiple_of((lax.rem(z, 2) * 4 + x * 8) * D, WIDTH), WIDTH)


def pair_table(z, y, x, c, docs, mask, order):
    z_hi = lax.div(z, 2)
    row = lax.broadcasted_iota(jnp.int32, (T, T), 0)
    col = lax.broadcasted_iota(jnp.int32, (T, T), 1)
    doc_cols = jnp.broadcast_to(docs[...].astype(F32), (T, T))
    live = (mask[...] == 1) & (doc_cols.T == doc_cols) & (row >= col)
    live = jnp.where(live, 1.0, 0.0).astype(BF16)
    holds = jnp.where(row == jnp.broadcast_to(order[...], (T, T)), 1.0, 0.0).astype(BF16)
    by_key = jnp.dot(live, holds, preferred_element_type=F32).astype(BF16)
    stored = lax.dot_general(holds, by_key, TN, preferred_element_type=F32).astype(BF16)
    small_row = lax.broadcasted_iota(jnp.int32, (QUERY_TILES, T), 0)
    small_col = lax.broadcasted_iota(jnp.int32, (QUERY_TILES, T), 1)
    first = (z_hi * 4 + y) * QUERY_TILES
    pick = jnp.where(small_col == small_row + first, 1.0, 0.0).astype(BF16)
    mine = jnp.dot(pick, stored, preferred_element_type=F32).astype(BF16)
    slot_z, slot_y, slot_x = col // 16, col // 4 % 4, col % 4
    source = (slot_z // 2) * 64 + slot_y * 16 + c * 8 + slot_z % 2 * 4 + slot_x
    spread = jnp.where((row == source) & (col < KEY_TILES), 1.0, 0.0).astype(BF16)
    pairs = jnp.dot(mine, spread, preferred_element_type=F32)
    own = ((z_hi * 2 + small_row % 8 // 4) * 4 + y) * 4 + small_row % 4
    is_own = (small_col == own) & (small_row // 8 == c)
    diag = jnp.sum(jnp.where(is_own, pairs, 0.0), axis=1, keepdims=True)
    rest = jnp.where(is_own, 0.0, pairs)
    upto = jnp.where(row <= col, 1.0, 0.0).astype(BF16)
    rank = jnp.dot(rest.astype(BF16), upto, preferred_element_type=F32)
    count = jnp.sum(rest, axis=1, keepdims=True)
    numbers = lax.broadcasted_iota(jnp.int32, (8, T), 1).astype(F32).astype(BF16)
    lists = []
    for i in range(QUERY_TILES):
        at = jnp.where(rest[i : i + 1, :] > 0.5, rank[i : i + 1, :] - 1.0, -1.0)
        chosen = jnp.where(jnp.broadcast_to(at, (T, T)) == row.astype(F32), 1.0, 0.0).astype(BF16)
        lists.append(lax.dot_general(numbers, chosen, NT, preferred_element_type=F32)[:1])
    table = jnp.concatenate(lists, axis=0)
    table = jnp.where(small_col == KEY_TILES, count, table)
    table = jnp.where(small_col == KEY_TILES + 1, diag, table)
    table = table.astype(jnp.int32)
    return jnp.where(small_col == KEY_TILES + 2, jnp.where(small_row // 8 == c, own, 0), table)


def gather(
    queries, grad_out, keys, values, attn_out, log_sums, key_gain, value_gain, docs, mask, order,
    qg, gg, kg, vg, stats, table,
    own_grad, key_parts, value_parts, stat_parts, sends, recvs, local,
):
    z, y, x, c = place()
    ka = lax.rem(z, 2) * 4 + x
    columns = head_columns(z, x)
    own_rows = pl.ds(pl.multiple_of(ka * T, T), T)
    locals_ = [
        pltpu.make_async_copy(grad_out.at[own_rows], own_grad, local.at[0]),
        pltpu.make_async_copy(queries.at[:, columns], qg.at[c], local.at[1]),
        pltpu.make_async_copy(grad_out.at[:, columns], gg.at[c], local.at[2]),
    ]
    for copy in locals_:
        copy.start()
    for j in range(RING):
        lanes = pl.ds(j * D, D)
        key_parts[j] = (keys[:, lanes].astype(F32) * key_gain[:, lanes]).astype(BF16)
        value_parts[j] = (values[:, lanes].astype(F32) * value_gain[:, lanes]).astype(BF16)

    peers = group_peers(z, y, x, c)
    y_plus, y_minus = ident(z, wrap(y + 1), x, c), ident(z, wrap(y - 1), x, c)
    z_plus, z_minus = ident(wrap(z + 1), y, x, c), ident(wrap(z - 1), y, x, c)
    far = ident(wrap(z + 2 * lax.rem(z, 2) - 1), y, x, c)
    greet([peer for _, _, peer in peers] + [y_plus, y_minus, far])

    slot = pl.ds(pl.multiple_of(x * T, T), T)
    across = Lane(sends, recvs, 0)
    for step in range(1, RING):
        to = wrap(x + step)
        across.send(key_parts.at[to], kg.at[z, y, slot], step - 1, ident(z, y, to, c))
        across.send(value_parts.at[to], vg.at[z, y, slot], step + 2, ident(z, y, to, c))
    kept = [
        pltpu.make_async_copy(key_parts.at[x], kg.at[z, y, slot], local.at[3]),
        pltpu.make_async_copy(value_parts.at[x], vg.at[z, y, slot], local.at[4]),
    ]
    for copy in kept:
        copy.start()
    sibling = ident(z, y, x, 1 - c)
    pair = Lane(sends, recvs, 6)
    pair.send(queries.at[:, columns], qg.at[c], 0, sibling)
    pair.send(grad_out.at[:, columns], gg.at[c], 1, sibling)

    locals_[0].wait()
    for to in range(KA):
        first = to % 4 * 8 + to // 4 * 4
        stat_parts[to, 0:HEADS, :] = log_sums[first : first + HEADS, :]
        for h in range(HEADS):
            lanes = pl.ds((first + h) * D, D)
            product = own_grad[:, lanes].astype(F32) * attn_out[:, lanes].astype(F32)
            stat_parts[to, HEADS + h : HEADS + h + 1, :] = jnp.sum(product.T, axis=0, keepdims=True)
    share = Lane(sends, recvs, 8)
    for flip, step, peer in peers:
        share.send(stat_parts.at[lax.rem(ka + step, KA)], stats.at[c * KA + ka], flip * KA + step, peer)
    keep_stats = pltpu.make_async_copy(stat_parts.at[ka], stats.at[c * KA + ka], local.at[5])
    keep_stats.start()

    for copy in kept:
        copy.wait()
    for step in range(1, RING):
        origin = wrap(x - step)
        came = pl.ds(pl.multiple_of(origin * T, T), T)
        across.arrive(kg.at[z, y, came], step - 1, ident(z, y, origin, c))
        across.arrive(vg.at[z, y, came], step + 2, ident(z, y, origin, c))

    def block(ref, dz, dy):
        return ref.at[wrap(z + dz), wrap(y + dy)]

    base = 24
    key_first = Spread(sends, recvs, base).setup(lambda o: block(kg, o, 0), z_plus, z_minus)
    value_first = Spread(sends, recvs, base + 4).setup(lambda o: block(vg, 0, o), y_plus, y_minus)
    key_then, value_then = {}, {}
    for n, off in enumerate((0, -1, 1, 2)):
        key_then[off] = Spread(sends, recvs, base + 8 + 4 * n).setup(
            lambda o, off=off: block(kg, off, o), y_plus, y_minus
        )
        value_then[off] = Spread(sends, recvs, base + 24 + 4 * n).setup(
            lambda o, off=off: block(vg, o, off), z_plus, z_minus
        )
    key_first.start()
    value_first.start()
    key_then[0].start()
    value_then[0].start()

    table[...] = pair_table(z, y, x, c, docs, mask, order)

    key_first.relay_up()
    value_first.relay_up()
    key_then[-1].start()
    value_then[-1].start()
    key_first.relay_down()
    value_first.relay_down()
    key_then[1].start()
    value_then[1].start()
    for off in (0,):
        key_then[off].relay_up()
        value_then[off].relay_up()
        key_then[off].relay_down()
        value_then[off].relay_down()
    key_first.finish()
    value_first.finish()
    key_then[2].start()
    value_then[2].start()
    for off in (-1, 1, 2):
        key_then[off].relay_up()
        value_then[off].relay_up()
        key_then[off].relay_down()
        value_then[off].relay_down()
    for off in (0, -1, 1, 2):
        key_then[off].finish()
        value_then[off].finish()

    pair.arrive(qg.at[1 - c], 0, sibling)
    pair.arrive(gg.at[1 - c], 1, sibling)
    for flip, step, _ in peers:
        origin = lax.rem(ka + KA - step, KA)
        core = 1 - c if flip else c
        from_ = ident(lax.div(z, 2) * 2 + lax.div(origin, 4), y, lax.rem(origin, 4), core)
        share.arrive(stats.at[core * KA + origin], flip * KA + step, from_)
    keep_stats.wait()
    for copy in locals_[1:]:
        copy.wait()
    for lane in [across, pair, share, key_first, value_first, *key_then.values(), *value_then.values()]:
        lane.drain()


def attend(table, stats, q_ref, g_ref, k_ref, v_ref, dq_ref, dk_ref, dv_ref, plan, dk_acc, dv_acc, dq_acc, held):
    scale = D ** -0.5

    dk_acc[...] = jnp.zeros_like(dk_acc)
    dv_acc[...] = jnp.zeros_like(dv_acc)
    dq_acc[...] = jnp.zeros_like(dq_acc)

    def stack(ref, i):
        rows = pl.ds(pl.multiple_of(i * T, T), T)
        return jnp.concatenate([ref[rows, h * D : (h + 1) * D] for h in range(HEADS)], axis=0)

    def tiles(ref, a, b):
        parts = [ref[pl.ds(pl.multiple_of(at * T, T), T), :] for at in (a, b)]
        return jnp.concatenate(parts, axis=0)

    def unpack(step):
        word = plan[step]
        return word >> 16, (word >> 8) & 63, word & 63, (word >> 14) & 1, (word >> 6) & 1

    def front(step, slot, masked):
        i, a, b, use_a, use_b = unpack(step)
        s = lax.dot_general(tiles(k_ref, a, b), stack(q_ref, i), NT, preferred_element_type=F32)
        dp = lax.dot_general(tiles(v_ref, a, b), stack(g_ref, i), NT, preferred_element_type=F32)
        lse = jnp.concatenate([stats[i, h : h + 1, :] for h in range(HEADS)], axis=1) * LOG2E
        delta = jnp.concatenate([stats[i, HEADS + h : HEADS + h + 1, :] for h in range(HEADS)], axis=1)
        p = jnp.exp2(s * (scale * LOG2E) - lse)
        if masked:
            row = lax.broadcasted_iota(jnp.int32, (T, T), 0)
            col = lax.broadcasted_iota(jnp.int32, (T, T), 1)
            ok_a = row < use_a * T
            ok_b = row <= col - (1 - use_b) * T
            ok = jnp.concatenate(
                [jnp.concatenate([ok_a] * HEADS, axis=1), jnp.concatenate([ok_b] * HEADS, axis=1)], axis=0
            )
            p = jnp.where(ok, p, 0.0)
        held[slot, 0] = p.astype(BF16)
        held[slot, 1] = (p * (dp - delta)).astype(BF16)

    def back(step, slot):
        i, a, b, _, _ = unpack(step)
        p, ds = held[slot, 0], held[slot, 1]
        dv = jnp.dot(p, stack(g_ref, i), preferred_element_type=F32)
        dk = jnp.dot(ds, stack(q_ref, i), preferred_element_type=F32)
        dq_acc[i] += lax.dot_general(tiles(k_ref, a, b), ds, TN, preferred_element_type=F32)
        for n, at in enumerate((a, b)):
            rows = pl.ds(pl.multiple_of(at * T, T), T)
            dv_acc[rows, :] += dv[n * T : (n + 1) * T]
            dk_acc[rows, :] += dk[n * T : (n + 1) * T]

    def run(steps, masked):
        plan[steps] = 0
        front(0, 0, masked)
        twos = lax.div(steps, 2)

        @pl.loop(0, twos)
        def _(u):
            front(2 * u + 1, 1, masked)
            back(2 * u, 0)
            front(2 * u + 2, 0, masked)
            back(2 * u + 1, 1)

        @pl.when(steps > 2 * twos)
        def _():
            back(steps - 1, 0)

    def list_whole(i, n):
        halves = lax.div(table[i, KEY_TILES], 2)

        def put(r, n):
            plan[n] = (i << 16) | (table[i, 2 * r] << 8) | table[i, 2 * r + 1]
            return n + 1

        return lax.fori_loop(0, halves, put, n)

    run(lax.fori_loop(0, QUERY_TILES, list_whole, jnp.int32(0)), False)

    def list_masked(i, n):
        count, diag = table[i, KEY_TILES], table[i, KEY_TILES + 1]
        odd = lax.rem(count, 2)
        last = table[i, jnp.maximum(count - 1, 0)]

        @pl.when(odd + diag > 0)
        def _():
            plan[n] = (i << 16) | (odd << 14) | (last << 8) | (diag << 6) | table[i, KEY_TILES + 2]

        return n + jnp.minimum(odd + diag, 1)

    run(lax.fori_loop(0, QUERY_TILES, list_masked, jnp.int32(0)), True)

    @pl.loop(0, QUERY_TILES)
    def _(i):
        rows = pl.ds(pl.multiple_of(i * T, T), T)
        for h in range(HEADS):
            lanes = slice(h * D, (h + 1) * D)
            dq_ref[rows, lanes] = (dq_acc[i, :, lanes].T * scale).astype(BF16)

    @pl.loop(0, KEY_TILES)
    def _(n):
        at = pl.ds(pl.multiple_of(n * T, T), T)
        dk_ref[at, :] = (dk_acc[at, :] * scale).astype(BF16)
        swapped = (lax.rem(lax.div(n, 4), 4) * 4 + lax.div(n, 16)) * 4 + lax.rem(n, 4)
        dv_ref[pl.ds(pl.multiple_of(swapped * T, T), T), :] = dv_acc[at, :].astype(BF16)


def scatter(
    dq, dk_whole, dv_whole, keys, values, key_gain, value_gain,
    grad_queries, grad_keys, grad_values, gains,
    dk, dv, dq_own, local, dq_in, land_k1, land_v1, land_k2, land_v2, parts, near, sums, total, sends, recvs,
):
    z, y, x, c = place()
    ka = lax.rem(z, 2) * 4 + x
    z_hi, z_lo = lax.div(z, 2), lax.rem(z, 2)
    own_block = pl.ds(pl.multiple_of(c * KA * T, KA * T), KA * T)
    loads = [
        pltpu.make_async_copy(dk_whole, dk, local.at[0]),
        pltpu.make_async_copy(dv_whole, dv, local.at[1]),
        pltpu.make_async_copy(dq.at[own_block], dq_own, local.at[2]),
    ]
    for copy in loads:
        copy.start()
    peers = group_peers(z, y, x, c)
    y_plus, y_minus = ident(z, wrap(y + 1), x, c), ident(z, wrap(y - 1), x, c)
    z_plus, z_minus = ident(wrap(z + 1), y, x, c), ident(wrap(z - 1), y, x, c)
    far = ident(wrap(z + 2 * z_lo - 1), y, x, c)
    others = []
    for flip in range(2):
        for step in range(RING):
            if flip or step:
                hi = 1 - z_hi if flip else z_hi
                others.append((flip, step, ident(hi * 2 + z_lo, wrap(y + step), x, c)))
    greet([peer for _, _, peer in peers] + [other for _, _, other in others] + [far])

    sibling = ident(z, y, x, 1 - c)
    pair = Lane(sends, recvs, 0)
    for n in range(KA):
        rows = pl.ds(pl.multiple_of((1 - c) * KA * T + n * T, T), T)
        pair.send(dq.at[rows], dq_in.at[n], n, sibling)

    half = 2 * RING * T

    def key_half(off, n):
        return dk.at[pl.ds(pl.multiple_of(wrap(z + off) * 4 * RING * T + n * 2 * RING * T, half), half)]

    def value_half(off, n):
        return dv.at[pl.ds(pl.multiple_of(wrap(y + off) * 4 * RING * T + n * 2 * RING * T, half), half)]

    key_first = Fold(sends, recvs, 16).setup(key_half, None, land_k1, z_plus, z_minus)
    value_first = Fold(sends, recvs, 22).setup(value_half, None, land_v1, y_plus, y_minus)
    loads[0].wait()
    key_first.start()
    loads[1].wait()
    value_first.start()
    loads[2].wait()

    lane_q = Lane(sends, recvs, 8)
    columns = head_columns(z, x)
    for n in range(KA):
        to = lax.rem(ka + n, KA)
        own_rows = dq_own.at[pl.ds(pl.multiple_of(to * T, T), T)]
        if n == 0:
            for m in range(KA):
                pair.arrive(dq_in.at[m], m, sibling)
        for h in range(HEADS):
            lanes = pl.ds(h * D, D)
            value = own_rows[:, lanes].astype(F32) + dq_in[to, :, lanes].astype(F32)
            dq_in[to, :, lanes] = value.astype(BF16)
        if n:
            peer = ident(z_hi * 2 + lax.div(to, 4), y, lax.rem(to, 4), c)
            lane_q.send(dq_in.at[to], grad_queries.at[:, columns], n, peer)
    grad_queries[:, columns] = dq_in[ka]

    key_first.relay()
    value_first.relay()
    key_first.finish()
    value_first.finish()

    def key_quarter(off, n):
        start = wrap(z) * 4 * RING * T + wrap(y + off) * RING * T + n * 2 * T
        return dk.at[pl.ds(pl.multiple_of(start, 2 * T), 2 * T)]

    def value_quarter(off, n):
        start = wrap(y) * 4 * RING * T + wrap(z + off) * RING * T + n * 2 * T
        return dv.at[pl.ds(pl.multiple_of(start, 2 * T), 2 * T)]

    key_then = Fold(sends, recvs, 28).setup(key_quarter, None, land_k2, y_plus, y_minus)
    value_then = Fold(sends, recvs, 34).setup(value_quarter, None, land_v2, z_plus, z_minus)
    key_then.start()
    value_then.start()
    key_then.relay()
    value_then.relay()
    key_then.finish()
    value_then.finish()

    across = Lane(sends, recvs, 40)
    block_k = pl.multiple_of((z * 4 + y) * RING * T, RING * T)
    block_v = pl.multiple_of((y * 4 + z) * RING * T, RING * T)
    for step in range(1, RING):
        to = wrap(x + step)
        across.send(dk.at[pl.ds(block_k + to * T, T)], parts.at[0, x], step - 1, ident(z, y, to, c))
        across.send(dv.at[pl.ds(block_v + to * T, T)], parts.at[1, x], step + 2, ident(z, y, to, c))
    parts[0, x] = dk[pl.ds(block_k + x * T, T), :]
    parts[1, x] = dv[pl.ds(block_v + x * T, T), :]
    for step in range(1, RING):
        origin = wrap(x - step)
        across.arrive(parts.at[0, origin], step - 1, ident(z, y, origin, c))
        across.arrive(parts.at[1, origin], step + 2, ident(z, y, origin, c))
    for n in range(RING):
        lanes = pl.ds(n * D, D)
        dkey, dvalue = parts[0, n].astype(F32), parts[1, n].astype(F32)
        grad_keys[:, lanes] = (dkey * key_gain[:, lanes]).astype(BF16)
        grad_values[:, lanes] = (dvalue * value_gain[:, lanes]).astype(BF16)
        sums[n : n + 1, :] = jnp.sum(dkey * keys[:, lanes].astype(F32), axis=0, keepdims=True)
        sums[4 + n : 5 + n, :] = jnp.sum(dvalue * values[:, lanes].astype(F32), axis=0, keepdims=True)

    mine = c * KA + ka
    share = Lane(sends, recvs, 46)
    for flip, step, peer in peers:
        share.send(sums, near.at[mine], flip * KA + step, peer)
    near[mine] = sums[...]
    for flip, step, _ in peers:
        origin = lax.rem(ka + KA - step, KA)
        core = 1 - c if flip else c
        from_ = ident(z_hi * 2 + lax.div(origin, 4), y, lax.rem(origin, 4), core)
        share.arrive(near.at[core * KA + origin], flip * KA + step, from_)
    total[0] = jnp.sum(near[...], axis=0)
    spread = Lane(sends, recvs, 62)
    mine = z_hi * RING + y
    for flip, step, other in others:
        spread.send(total.at[0], total.at[1 + mine], flip * RING + step, other)
    total[1 + mine] = total[0]
    for flip, step, _ in others:
        hi = 1 - z_hi if flip else z_hi
        origin = wrap(y - step)
        spread.arrive(total.at[1 + hi * RING + origin], flip * RING + step, ident(hi * 2 + z_lo, origin, x, c))
    gains[...] = jnp.sum(total[1:], axis=0)

    for n in range(1, KA):
        origin = lax.rem(ka + KA - n, KA)
        their = head_columns(lax.div(origin, 4), lax.rem(origin, 4))
        from_ = ident(z_hi * 2 + lax.div(origin, 4), y, lax.rem(origin, 4), c)
        lane_q.arrive(grad_queries.at[:, their], n, from_)
    for lane in [pair, lane_q, key_first, value_first, key_then, value_then, across, share, spread]:
        lane.drain()


def shape(dims, dtype):
    return jax.ShapeDtypeStruct(dims, dtype)


def shards(
    queries, key_rows, values, attn_out, grad_out, log_sums, key_gain, value_gain, doc_ids, tile_mask, block_order
):
    vm, hbm = pl.BlockSpec(memory_space=pltpu.VMEM), pl.BlockSpec(memory_space=pl.ANY)
    key_gain, value_gain = key_gain.reshape(1, -1), value_gain.reshape(1, -1)
    rows = queries.shape[0]
    qg, gg, kg, vg, stats, table = pl.pallas_call(
        gather,
        out_shape=(
            shape((2, rows, WIDTH), BF16),
            shape((2, rows, WIDTH), BF16),
            shape((RING, RING, RING * T, D), BF16),
            shape((RING, RING, RING * T, D), BF16),
            shape((QUERY_TILES, 2 * HEADS, T), F32),
            shape((QUERY_TILES, T), jnp.int32),
        ),
        in_specs=[hbm, hbm] + [vm] * 9,
        out_specs=(hbm, hbm, hbm, hbm, hbm, vm),
        scratch_shapes=[
            pltpu.VMEM(attn_out.shape, BF16),
            pltpu.VMEM((RING, T, D), BF16),
            pltpu.VMEM((RING, T, D), BF16),
            pltpu.VMEM((KA, 2 * HEADS, T), F32),
            pltpu.SemaphoreType.DMA((64,)),
            pltpu.SemaphoreType.DMA((64,)),
            pltpu.SemaphoreType.DMA((6,)),
        ],
        compiler_params=pltpu.CompilerParams(
            collective_id=0, has_side_effects=True, vmem_limit_bytes=32 * 2**20
        ),
        name="gather",
    )(
        queries, grad_out, key_rows, values, attn_out, log_sums, key_gain, value_gain,
        doc_ids.reshape(1, -1), tile_mask, block_order.reshape(1, -1),
    )
    dq, dk, dv = pl.pallas_call(
        attend,
        out_shape=(
            shape((2 * rows, WIDTH), BF16),
            shape((KEY_TILES * T, D), BF16),
            shape((KEY_TILES * T, D), BF16),
        ),
        in_specs=[pl.BlockSpec(memory_space=pltpu.SMEM)] + [vm] * 5,
        out_specs=(vm, vm, vm),
        scratch_shapes=[
            pltpu.SMEM((QUERY_TILES * KEY_TILES // 2 + 2,), jnp.int32),
            pltpu.VMEM((KEY_TILES * T, D), F32),
            pltpu.VMEM((KEY_TILES * T, D), F32),
            pltpu.VMEM((QUERY_TILES, D, WIDTH), F32),
            pltpu.VMEM((2, 2, 2 * T, WIDTH), BF16),
        ],
        compiler_params=pltpu.CompilerParams(vmem_limit_bytes=56 * 2**20),
        name="attend",
    )(
        table, stats, qg.reshape(2 * rows, WIDTH), gg.reshape(2 * rows, WIDTH),
        kg.reshape(KEY_TILES * T, D), vg.reshape(KEY_TILES * T, D),
    )
    grad_queries, grad_keys, grad_values, gains = pl.pallas_call(
        scatter,
        out_shape=(
            shape(attn_out.shape, BF16),
            shape(key_rows.shape, BF16),
            shape(values.shape, BF16),
            shape((2 * RING, D), F32),
        ),
        in_specs=[hbm] * 3 + [vm] * 4,
        out_specs=(vm, vm, vm, vm),
        scratch_shapes=[
            pltpu.VMEM((KEY_TILES * T, D), BF16),
            pltpu.VMEM((KEY_TILES * T, D), BF16),
            pltpu.VMEM((rows, WIDTH), BF16),
            pltpu.SemaphoreType.DMA((3,)),
            pltpu.VMEM((KA, T, WIDTH), BF16),
            pltpu.VMEM((6, 2 * RING * T, D), BF16),
            pltpu.VMEM((6, 2 * RING * T, D), BF16),
            pltpu.VMEM((6, 2 * T, D), BF16),
            pltpu.VMEM((6, 2 * T, D), BF16),
            pltpu.VMEM((2, RING, T, D), BF16),
            pltpu.VMEM((QUERY_TILES, 2 * RING, D), F32),
            pltpu.VMEM((2 * RING, D), F32),
            pltpu.VMEM((9, 2 * RING, D), F32),
            pltpu.SemaphoreType.DMA((70,)),
            pltpu.SemaphoreType.DMA((70,)),
        ],
        compiler_params=pltpu.CompilerParams(
            collective_id=1, has_side_effects=True, vmem_limit_bytes=48 * 2**20
        ),
        name="scatter",
    )(dq, dk, dv, key_rows, values, key_gain, value_gain)
    return grad_queries, grad_keys, grad_values, gains[:RING].reshape(-1), gains[RING:].reshape(-1)


def solution(mesh):
    rows = P(("pb", "ka"), None)
    placed = (P("pb", None), rows, rows, rows, P("pb", None), P(None, ("pb", "ka")), P(), P(), P(), P(), P())
    return jax.shard_map(
        shards, mesh=mesh, in_specs=placed, out_specs=(rows, rows, rows, P(), P()), check_vma=False
    )
```

time: 1520 us -> 177 us (0.12)
  waiting for transfers between devices: 955 us -> 0 us
  local copies, waits for them, and re-layouts: 222 us -> 23.3 us
  blocking collectives: 185 us -> 0 us
  Pallas kernels: 0 us -> 153 us
  loops' own time: 49.4 us -> 0 us
  other arithmetic: 47.6 us -> 0 us
  matrix products: 31.2 us -> 0 us
    reduce_scatter x3 -> x0, waiting for transfers between devices: 910 us -> none  [the longest x1 828 us: shards(): lax.psum_scatter(value_sum, 'pb', scatter_dimension=0, tiled=True)]
    pallas_call x0 -> x3, Pallas kernels: none -> 153 us  [the longest x1 64.1 us: shards(): pl.pallas_call(scatter, out_shape=(shape(attn_out.shape, BF16), shape(key...]
    psum x1 -> x0, blocking collectives: 138 us -> none  [shards(): lax.psum((jnp.sum(key_mine * key_rows.astype(jnp.float32), axis=0), jnp.s...]
    dynamic_slice x120 -> x0, local copies, waits for them, and re-layouts: 121 us -> none  [the longest x50 56.2 us: add_rows(): current = lax.dynamic_slice_in_dim(total, start, term.shape[0], 0)]
    dynamic_update_slice x60 -> x0, local copies, waits for them, and re-layouts: 67.9 us -> none  [add_rows(): return lax.dynamic_update_slice_in_dim(total, current + term, start, 0)]
    another operation x1 -> x0, loops' own time: 49.4 us -> none  [shards(): lax.fori_loop(loop_start, live_count, joint_step, (empty_query, empty_key...]
    all_gather x2 -> x0, blocking collectives: 46.9 us -> none  [the longest x1 24.2 us: shards(): lax.all_gather(delta_own, 'ka', axis=1, tiled=True)]
    all_gather x2 -> x0, waiting for transfers between devices: 45 us -> none  [the longest x1 45 us: shards(): lax.all_gather(values, 'pb', axis=0, tiled=True)]
  transfers between devices with their start and end apart: 5 -> 0, of which waited for: 3 -> 0; matrix products, arithmetic and copies ran while one was open for 2% -> 0% of each run, Pallas kernels for 0% -> 0%
where the time goes in v1:
time: 177 us
  Pallas kernels  153 us (86%)
  local copies, waits for them, and re-layouts  23.3 us (13%)
    pallas_call x1, Pallas kernels, shards(): pl.pallas_call(scatter, out_shape=(shape(attn_out.shape, BF16), shape(key...  64.1 us
    pallas_call x1, Pallas kernels, shards(): pl.pallas_call(attend, out_shape=(shape((2 * rows, WIDTH), BF16), shape((...  52.9 us
    pallas_call x1, Pallas kernels, shards(): pl.pallas_call(gather, out_shape=(shape((2, rows, WIDTH), BF16), shape((2...  36.1 us
    unnamed x47, local copies, waits for them, and re-layouts  22.7 us

profile of v1, /device:TPU:1, one launch (start us, length us, event | category | flops | bytes accessed | tf_op | source)
XLA Modules:
  0.0 177.0 jit_solution(17235249685057399129)
XLA Ops:
  0.6 3.4 %copy-done = bf16[1024,4096]{1,0:T(8,128)(2,1)S(1)} copy-done((bf16[1024,4096]{1,0:T(8,128)(2,1)S(1)}, bf16[1024,4096]{1,0:T(8,128)(2,1)}, u32[]{:S(2)}) %copy-start) | copy-done | bytes 8388632
  4.0 1.2 copy-done.7
  5.2 0.9 copy-done.8
  6.1 0.9 copy-done.10
  7.1 0.8 copy-done.12
  7.9 0.7 copy-done.14
  8.6 0.7 copy-done.16
  9.3 0.7 copy-done.18
  10.0 0.7 copy-done.20
  10.6 0.7 copy-done.21
  11.3 36.1 %gather.1 = (bf16[2,1024,512]{2,1,0:T(8,128)(2,1)S(1)}, bf16[2,1024,512]{2,1,0:T(8,128)(2,1)S(1)}, bf16[4,4,512,128]{3,2,1,0:T(8,128)(2,1)S(1)}, bf16[4,4,512,12...) custom-call(bf16[1024,4096]{1,0:T(8,128)(2,1)S(1)} %copy-done, ...), custom_call_target="tpu_custom_call" | custom-call | tf_op jit(solution)/shard_map/gather/pallas_call | solution.py:585
  47.4 1.3 copy-done.1
  48.7 1.3 copy-done.2
  50.0 1.3 copy-done.3
  51.4 1.4 copy-done.4
  52.7 0.6 copy-done.13
  53.4 0.6 copy-done.15
  54.0 52.9 %attend.1 = (bf16[2048,512]{1,0:T(8,128)(2,1)}, bf16[8192,128]{1,0:T(8,128)(2,1)}, bf16[8192,128]{1,0:T(8,128)(2,1)}) custom-call(s32[16,128]{1,0:T(8,128)} %copy-done.15, f32[16,8,128]{2,1,0:T(8,128)} %copy-done.13, bf16[2048,512]{1,0:T(8,128)(2,1)} %bitcast.12, bf16[2048,512]{1,0:T(8,128)(2,1)} %bitcast.13, bf16[8192,128]{1,0:T(8,128)(2,1)} %bitcast.14, ...), custom_call_target="tpu_custom_call" | custom-call | tf_op jit(solution)/shard_map/attend/pallas_call | solution.py:614
  106.9 1.6 copy-done.5
  108.5 1.6 copy-done.6
  110.0 64.1 %scatter.1 = (bf16[128,4096]{1,0:T(8,128)(2,1)S(1)}, bf16[128,512]{1,0:T(8,128)(2,1)S(1)}, bf16[128,512]{1,0:T(8,128)(2,1)S(1)}, f32[8,128]{1,0:T(8,128)S(1)}) custom-call(bf16[2048,512]{1,0:T(8,128)(2,1)S(1)} %copy-done.5, bf16[8192,128]{1,0:T(8,128)(2,1)S(1)} %copy-done.6, bf16[8192,128]{1,0:T(8,128)(2,1)} %get-tuple-element.26.dv_whole, ...), custom_call_target="tpu_custom_call" | custom-call | tf_op jit(solution)/shard_map/scatter/pallas_call | solution.py:636
  174.8 1.0 copy.19
  175.7 0.7 copy.20
  176.4 0.7 copy.21
  (27 shorter events, 0.6 us)
Async XLA Ops:
  0.6 3.4 %copy-start = (bf16[1024,4096]{1,0:T(8,128)(2,1)S(1)}, bf16[1024,4096]{1,0:T(8,128)(2,1)}, u32[]{:S(2)}) copy-start(bf16[1024,4096]{1,0:T(8,128)(2,1)} %queries.1) | copy-start | bytes 25165828
  4.0 1.2 copy-start.7
  5.2 0.9 copy-start.8
  6.1 0.9 copy-start.10
  7.1 0.8 copy-start.12
  7.9 0.7 copy-start.14
  8.6 0.7 copy-start.16
  9.3 0.7 copy-start.18
  10.0 0.7 copy-start.20
  10.6 0.7 copy-start.21
  47.4 1.3 copy-start.1
  48.7 1.3 copy-start.2
  50.0 1.3 copy-start.3
  51.4 1.4 copy-start.4
  52.7 0.6 copy-start.13
  53.4 0.6 copy-start.15
  54.0 52.9 %copy-start.9 = (bf16[128,512]{1,0:T(8,128)(2,1)S(1)}, bf16[128,512]{1,0:T(8,128)(2,1)}, u32[]{:S(2)}) copy-start(bf16[128,512]{1,0:T(8,128)(2,1)} %keys.3) | copy-start | bytes 393220
  54.0 52.9 %copy-start.11 = (bf16[128,512]{1,0:T(8,128)(2,1)S(1)}, bf16[128,512]{1,0:T(8,128)(2,1)}, u32[]{:S(2)}) copy-start(bf16[128,512]{1,0:T(8,128)(2,1)} %values.3) | copy-start | bytes 393220
  54.0 52.9 %copy-start.17 = (f32[512]{0:T(512)S(1)}, f32[512]{0:T(512)}, u32[]{:S(2)}) copy-start(f32[512]{0:T(512)} %param.17) | copy-start | bytes 6148
  54.0 52.9 %copy-start.19 = (f32[512]{0:T(512)S(1)}, f32[512]{0:T(512)}, u32[]{:S(2)}) copy-start(f32[512]{0:T(512)} %param.18) | copy-start | bytes 6148
  106.9 1.6 copy-start.5
  108.4 1.6 copy-start.6

commit v2 on v1

--- a/solution.py
+++ b/solution.py
@@ -118,8 +118,8 @@
 
 
 class Fold(Lane):
-    def setup(self, half_of, put, land, plus, minus):
-        self.half_of, self.put, self.land, self.plus, self.minus = half_of, put, land, plus, minus
+    def setup(self, half_of, land, plus, minus):
+        self.half_of, self.land, self.plus, self.minus = half_of, land, plus, minus
         return self
 
     def start(self):
@@ -130,31 +130,63 @@
 
     def relay(self):
         self.arrive(self.land.at[0], 0, self.minus)
-        add_into(self.half_of(1, 0), [self.land.at[0]])
-        self.send(self.half_of(1, 0), self.land.at[2], 2, self.plus)
+        combine(self.land.at[0], [self.land.at[0], self.half_of(1, 0)])
+        self.send(self.land.at[0], self.land.at[2], 2, self.plus)
         self.arrive(self.land.at[1], 1, self.plus)
-        add_into(self.half_of(-1, 1), [self.land.at[1]])
-        self.send(self.half_of(-1, 1), self.land.at[5], 5, self.minus)
-
-    def finish(self):
+        combine(self.land.at[1], [self.land.at[1], self.half_of(-1, 1)])
+        self.send(self.land.at[1], self.land.at[5], 5, self.minus)
+
+    def finish(self, factor=None):
         self.arrive(self.land.at[3], 3, self.minus)
         self.arrive(self.land.at[4], 4, self.plus)
         self.arrive(self.land.at[2], 2, self.minus)
-        add_into(self.half_of(0, 0), [self.land.at[2], self.land.at[4]])
+        combine(self.land.at[2], [self.half_of(0, 0), self.land.at[2], self.land.at[4]], factor)
         self.arrive(self.land.at[5], 5, self.plus)
-        add_into(self.half_of(0, 1), [self.land.at[3], self.land.at[5]])
-
-
-def add_into(total, terms):
-    rows = 256
-
-    @pl.loop(0, total.shape[0] // rows)
+        combine(self.land.at[3], [self.half_of(0, 1), self.land.at[3], self.land.at[5]], factor)
+
+
+class Detour(Lane):
+    def setup(self, item, cuts, land, z, hi, lo):
+        self.item, self.cuts, self.land, self.z, self.hi, self.lo = item, cuts, land, z, hi, lo
+        side = 2 * lax.rem(z, 2) - 1
+        self.at_hi, self.at_lo, self.at_far = wrap(z + side), wrap(z - side), wrap(z + 2)
+        return self
+
+    def start(self):
+        for n, cut in enumerate(self.cuts):
+            self.send(self.item(self.at_far).at[cut], self.land.at[0].at[cut], n, self.hi)
+        self.send(self.item(self.at_hi), self.land.at[1], len(self.cuts), self.hi)
+
+    def relay(self, n):
+        cut = self.cuts[n]
+        passed = self.land.at[0].at[cut]
+        self.arrive(passed, n, self.hi)
+        combine(passed, [passed, self.item(self.at_lo).at[cut]])
+        self.send(passed, self.land.at[2].at[cut], len(self.cuts) + 1 + n, self.lo)
+
+    def finish(self, total, factor=None):
+        self.arrive(self.land.at[1], len(self.cuts), self.hi)
+        for n, cut in enumerate(self.cuts):
+            self.arrive(self.land.at[2].at[cut], len(self.cuts) + 1 + n, self.lo)
+        combine(total, [self.item(self.z), self.land.at[1], self.land.at[2]], factor)
+
+
+def combine(total, terms, factor=None):
+    lead = total.shape[:-2]
+
+    @pl.loop(0, math.prod(lead))
     def _(n):
-        at = pl.ds(pl.multiple_of(n * rows, rows), rows)
-        value = total[at, :].astype(F32)
-        for term in terms:
-            value = value + term[at, :].astype(F32)
-        total[at, :] = value.astype(total.dtype)
+        at = []
+        for extent in reversed(lead):
+            at.append(lax.rem(n, extent))
+            n = lax.div(n, extent)
+        at = tuple(reversed(at))
+        value = terms[0][at].astype(F32)
+        for term in terms[1:]:
+            value = value + term[at].astype(F32)
+        if factor is not None:
+            value = value * factor
+        total[at] = value.astype(total.dtype)
 
 
 def head_columns(z, x):
@@ -201,25 +233,33 @@
 
 
 def gather(
-    queries, grad_out, keys, values, attn_out, log_sums, key_gain, value_gain, docs, mask, order,
-    qg, gg, kg, vg, stats, table,
-    own_grad, key_parts, value_parts, stat_parts, sends, recvs, local,
+    queries, grad_out, keys, values, attn_in, logs_in, docs_in, mask_in, order_in,
+    sibling_rows, kg, vg, stats, table_out,
+    table, attn_out, log_sums, docs, mask, order,
+    own_grad, stat_parts, sends, recvs, local,
 ):
     z, y, x, c = place()
     ka = lax.rem(z, 2) * 4 + x
     columns = head_columns(z, x)
     own_rows = pl.ds(pl.multiple_of(ka * T, T), T)
-    locals_ = [
-        pltpu.make_async_copy(grad_out.at[own_rows], own_grad, local.at[0]),
-        pltpu.make_async_copy(queries.at[:, columns], qg.at[c], local.at[1]),
-        pltpu.make_async_copy(grad_out.at[:, columns], gg.at[c], local.at[2]),
+    loads = [
+        pltpu.make_async_copy(source, target, local.at[6 + n])
+        for n, (source, target) in enumerate(
+            (
+                (attn_in, attn_out),
+                (logs_in, log_sums),
+                (docs_in, docs),
+                (mask_in, mask),
+                (order_in, order),
+            )
+        )
     ]
-    for copy in locals_:
+    loads.append(pltpu.make_async_copy(grad_out.at[own_rows], own_grad, local.at[0]))
+    for copy in loads:
         copy.start()
-    for j in range(RING):
-        lanes = pl.ds(j * D, D)
-        key_parts[j] = (keys[:, lanes].astype(F32) * key_gain[:, lanes]).astype(BF16)
-        value_parts[j] = (values[:, lanes].astype(F32) * value_gain[:, lanes]).astype(BF16)
+
+    def part(ref, to):
+        return ref.at[:, pl.ds(pl.multiple_of(to * D, D), D)]
 
     peers = group_peers(z, y, x, c)
     y_plus, y_minus = ident(z, wrap(y + 1), x, c), ident(z, wrap(y - 1), x, c)
@@ -231,32 +271,18 @@
     across = Lane(sends, recvs, 0)
     for step in range(1, RING):
         to = wrap(x + step)
-        across.send(key_parts.at[to], kg.at[z, y, slot], step - 1, ident(z, y, to, c))
-        across.send(value_parts.at[to], vg.at[z, y, slot], step + 2, ident(z, y, to, c))
+        across.send(part(keys, to), kg.at[z, y, slot], step - 1, ident(z, y, to, c))
+        across.send(part(values, to), vg.at[z, y, slot], step + 2, ident(z, y, to, c))
     kept = [
-        pltpu.make_async_copy(key_parts.at[x], kg.at[z, y, slot], local.at[3]),
-        pltpu.make_async_copy(value_parts.at[x], vg.at[z, y, slot], local.at[4]),
+        pltpu.make_async_copy(part(keys, x), kg.at[z, y, slot], local.at[3]),
+        pltpu.make_async_copy(part(values, x), vg.at[z, y, slot], local.at[4]),
     ]
     for copy in kept:
         copy.start()
     sibling = ident(z, y, x, 1 - c)
     pair = Lane(sends, recvs, 6)
-    pair.send(queries.at[:, columns], qg.at[c], 0, sibling)
-    pair.send(grad_out.at[:, columns], gg.at[c], 1, sibling)
-
-    locals_[0].wait()
-    for to in range(KA):
-        first = to % 4 * 8 + to // 4 * 4
-        stat_parts[to, 0:HEADS, :] = log_sums[first : first + HEADS, :]
-        for h in range(HEADS):
-            lanes = pl.ds((first + h) * D, D)
-            product = own_grad[:, lanes].astype(F32) * attn_out[:, lanes].astype(F32)
-            stat_parts[to, HEADS + h : HEADS + h + 1, :] = jnp.sum(product.T, axis=0, keepdims=True)
-    share = Lane(sends, recvs, 8)
-    for flip, step, peer in peers:
-        share.send(stat_parts.at[lax.rem(ka + step, KA)], stats.at[c * KA + ka], flip * KA + step, peer)
-    keep_stats = pltpu.make_async_copy(stat_parts.at[ka], stats.at[c * KA + ka], local.at[5])
-    keep_stats.start()
+    pair.send(queries.at[:, columns], sibling_rows.at[0], 0, sibling)
+    pair.send(grad_out.at[:, columns], sibling_rows.at[1], 1, sibling)
 
     for copy in kept:
         copy.wait()
@@ -285,7 +311,20 @@
     key_then[0].start()
     value_then[0].start()
 
-    table[...] = pair_table(z, y, x, c, docs, mask, order)
+    for copy in loads:
+        copy.wait()
+    for to in range(KA):
+        first = to % 4 * 8 + to // 4 * 4
+        stat_parts[to, 0:HEADS, :] = log_sums[first : first + HEADS, :]
+        for h in range(HEADS):
+            lanes = pl.ds((first + h) * D, D)
+            product = own_grad[:, lanes].astype(F32) * attn_out[:, lanes].astype(F32)
+            stat_parts[to, HEADS + h : HEADS + h + 1, :] = jnp.sum(product.T, axis=0, keepdims=True)
+    share = Lane(sends, recvs, 8)
+    for flip, step, peer in peers:
+        share.send(stat_parts.at[lax.rem(ka + step, KA)], stats.at[c * KA + ka], flip * KA + step, peer)
+    keep_stats = pltpu.make_async_copy(stat_parts.at[ka], stats.at[c * KA + ka], local.at[5])
+    keep_stats.start()
 
     key_first.relay_up()
     value_first.relay_up()
@@ -295,6 +334,9 @@
     value_first.relay_down()
     key_then[1].start()
     value_then[1].start()
+    table[...] = pair_table(z, y, x, c, docs, mask, order)
+    keep_table = pltpu.make_async_copy(table, table_out, local.at[11])
+    keep_table.start()
     for off in (0,):
         key_then[off].relay_up()
         value_then[off].relay_up()
@@ -313,23 +355,44 @@
         key_then[off].finish()
         value_then[off].finish()
 
-    pair.arrive(qg.at[1 - c], 0, sibling)
-    pair.arrive(gg.at[1 - c], 1, sibling)
+    pair.arrive(sibling_rows.at[0], 0, sibling)
+    pair.arrive(sibling_rows.at[1], 1, sibling)
     for flip, step, _ in peers:
         origin = lax.rem(ka + KA - step, KA)
         core = 1 - c if flip else c
         from_ = ident(lax.div(z, 2) * 2 + lax.div(origin, 4), y, lax.rem(origin, 4), core)
         share.arrive(stats.at[core * KA + origin], flip * KA + step, from_)
     keep_stats.wait()
-    for copy in locals_[1:]:
-        copy.wait()
+    keep_table.wait()
     for lane in [across, pair, share, key_first, value_first, *key_then.values(), *value_then.values()]:
         lane.drain()
 
 
-def attend(table, stats, q_ref, g_ref, k_ref, v_ref, dq_ref, dk_ref, dv_ref, plan, dk_acc, dv_acc, dq_acc, held):
+def attend(
+    table, stats_in, queries, grad_out, sibling_rows, keys_in, values_in, key_gain, value_gain,
+    dq_ref, dk_ref, dv_ref, gains,
+    plan, stats, q_ref, g_ref, keys, values, k_ref, v_ref, dk_acc, dv_acc, dq_acc, held, gain_acc, local,
+):
     scale = D ** -0.5
-
+    z, _, x, c = place()
+    columns = head_columns(z, x)
+    own, other = [pl.ds(pl.multiple_of(core * KA * T, KA * T), KA * T) for core in (c, 1 - c)]
+    loads = [
+        pltpu.make_async_copy(source, target, local.at[n])
+        for n, (source, target) in enumerate(
+            (
+                (keys_in, keys),
+                (values_in, values),
+                (stats_in, stats),
+                (queries.at[:, columns], q_ref.at[own]),
+                (grad_out.at[:, columns], g_ref.at[own]),
+                (sibling_rows.at[0], q_ref.at[other]),
+                (sibling_rows.at[1], g_ref.at[other]),
+            )
+        )
+    ]
+    for copy in loads:
+        copy.start()
     dk_acc[...] = jnp.zeros_like(dk_acc)
     dv_acc[...] = jnp.zeros_like(dv_acc)
     dq_acc[...] = jnp.zeros_like(dq_acc)
@@ -401,7 +464,20 @@
 
         return lax.fori_loop(0, halves, put, n)
 
-    run(lax.fori_loop(0, QUERY_TILES, list_whole, jnp.int32(0)), False)
+    steps = lax.fori_loop(0, QUERY_TILES, list_whole, jnp.int32(0))
+    lanes = pl.ds(pl.multiple_of(x * D, D), D)
+    for n, (raw, scaled, gain) in enumerate(((keys, k_ref, key_gain), (values, v_ref, value_gain))):
+        loads[n].wait()
+        factor = gain[:, lanes]
+
+        @pl.loop(0, KEY_TILES // 2)
+        def _(n):
+            at = pl.ds(pl.multiple_of(n * 2 * T, 2 * T), 2 * T)
+            scaled[at, :] = (raw[at, :].astype(F32) * factor).astype(BF16)
+
+    for copy in loads[2:]:
+        copy.wait()
+    run(steps, False)
 
     def list_masked(i, n):
         count, diag = table[i, KEY_TILES], table[i, KEY_TILES + 1]
@@ -423,30 +499,31 @@
             lanes = slice(h * D, (h + 1) * D)
             dq_ref[rows, lanes] = (dq_acc[i, :, lanes].T * scale).astype(BF16)
 
+    gain_acc[...] = jnp.zeros_like(gain_acc)
+
     @pl.loop(0, KEY_TILES)
     def _(n):
         at = pl.ds(pl.multiple_of(n * T, T), T)
-        dk_ref[at, :] = (dk_acc[at, :] * scale).astype(BF16)
-        swapped = (lax.rem(lax.div(n, 4), 4) * 4 + lax.div(n, 16)) * 4 + lax.rem(n, 4)
-        dv_ref[pl.ds(pl.multiple_of(swapped * T, T), T), :] = dv_acc[at, :].astype(BF16)
+        dkey, dvalue = dk_acc[at, :] * scale, dv_acc[at, :]
+        owner = (lax.div(n, 16), lax.rem(lax.div(n, 4), 4), lax.rem(n, 4))
+        dk_ref[owner] = dkey.astype(BF16)
+        dv_ref[owner] = dvalue.astype(BF16)
+        gain_acc[0] += jnp.sum((dkey * keys[at, :].astype(F32)).reshape(T // 8, 8, D), axis=0)
+        gain_acc[1] += jnp.sum((dvalue * values[at, :].astype(F32)).reshape(T // 8, 8, D), axis=0)
+
+    gains[...] = jnp.zeros_like(gains)
+    for n in range(2):
+        gains[n : n + 1, :] = jnp.sum(gain_acc[n], axis=0, keepdims=True)
 
 
 def scatter(
-    dq, dk_whole, dv_whole, keys, values, key_gain, value_gain,
-    grad_queries, grad_keys, grad_values, gains,
-    dk, dv, dq_own, local, dq_in, land_k1, land_v1, land_k2, land_v2, parts, near, sums, total, sends, recvs,
+    dq, dk, dv, partial, key_gain, value_gain,
+    grad_queries, grad_keys, grad_values, grad_key_gain, grad_value_gain,
+    dq_in, land_z, land_v, land_k, land_zy, land_vz, land_kz, final, near, total, sends, recvs,
 ):
     z, y, x, c = place()
     ka = lax.rem(z, 2) * 4 + x
     z_hi, z_lo = lax.div(z, 2), lax.rem(z, 2)
-    own_block = pl.ds(pl.multiple_of(c * KA * T, KA * T), KA * T)
-    loads = [
-        pltpu.make_async_copy(dk_whole, dk, local.at[0]),
-        pltpu.make_async_copy(dv_whole, dv, local.at[1]),
-        pltpu.make_async_copy(dq.at[own_block], dq_own, local.at[2]),
-    ]
-    for copy in loads:
-        copy.start()
     peers = group_peers(z, y, x, c)
     y_plus, y_minus = ident(z, wrap(y + 1), x, c), ident(z, wrap(y - 1), x, c)
     z_plus, z_minus = ident(wrap(z + 1), y, x, c), ident(wrap(z - 1), y, x, c)
@@ -459,33 +536,38 @@
                 others.append((flip, step, ident(hi * 2 + z_lo, wrap(y + step), x, c)))
     greet([peer for _, _, peer in peers] + [other for _, _, other in others] + [far])
 
+    spread = Lane(sends, recvs, 70)
+    mine = z_hi * RING + y
+    for flip, step, other in others:
+        spread.send(partial, total.at[mine], flip * RING + step, other)
+    total[mine] = partial[...]
+
     sibling = ident(z, y, x, 1 - c)
     pair = Lane(sends, recvs, 0)
     for n in range(KA):
         rows = pl.ds(pl.multiple_of((1 - c) * KA * T + n * T, T), T)
         pair.send(dq.at[rows], dq_in.at[n], n, sibling)
 
-    half = 2 * RING * T
-
-    def key_half(off, n):
-        return dk.at[pl.ds(pl.multiple_of(wrap(z + off) * 4 * RING * T + n * 2 * RING * T, half), half)]
-
-    def value_half(off, n):
-        return dv.at[pl.ds(pl.multiple_of(wrap(y + off) * 4 * RING * T + n * 2 * RING * T, half), half)]
-
-    key_first = Fold(sends, recvs, 16).setup(key_half, None, land_k1, z_plus, z_minus)
-    value_first = Fold(sends, recvs, 22).setup(value_half, None, land_v1, y_plus, y_minus)
-    loads[0].wait()
-    key_first.start()
-    loads[1].wait()
-    value_first.start()
-    loads[2].wait()
+    z_far, z_near = far, ident(wrap(z + 1 - 2 * z_lo), y, x, c)
+    some = pl.ds(0, RING - 1)
+    keys_z = Detour(sends, recvs, 16).setup(
+        lambda at: dk.at[at, :, some], [pl.ds(0, 2), pl.ds(2, 2)], land_z, z, z_far, z_near
+    )
+    values_y = Fold(sends, recvs, 22).setup(
+        lambda off, n: dv.at[pl.ds(2 * n, 2), wrap(y + off)], land_v, y_plus, y_minus
+    )
+    last_y = Fold(sends, recvs, 28).setup(
+        lambda off, n: dk.at[pl.ds(2 * n, 2), wrap(y + off), RING - 1], land_k, y_plus, y_minus
+    )
+    keys_z.start()
+    last_y.start()
+    values_y.start()
 
     lane_q = Lane(sends, recvs, 8)
     columns = head_columns(z, x)
     for n in range(KA):
         to = lax.rem(ka + n, KA)
-        own_rows = dq_own.at[pl.ds(pl.multiple_of(to * T, T), T)]
+        own_rows = dq.at[pl.ds(pl.multiple_of((c * KA + to) * T, T), T)]
         if n == 0:
             for m in range(KA):
                 pair.arrive(dq_in.at[m], m, sibling)
@@ -498,82 +580,109 @@
             lane_q.send(dq_in.at[to], grad_queries.at[:, columns], n, peer)
     grad_queries[:, columns] = dq_in[ka]
 
-    key_first.relay()
-    value_first.relay()
-    key_first.finish()
-    value_first.finish()
-
-    def key_quarter(off, n):
-        start = wrap(z) * 4 * RING * T + wrap(y + off) * RING * T + n * 2 * T
-        return dk.at[pl.ds(pl.multiple_of(start, 2 * T), 2 * T)]
-
-    def value_quarter(off, n):
-        start = wrap(y) * 4 * RING * T + wrap(z + off) * RING * T + n * 2 * T
-        return dv.at[pl.ds(pl.multiple_of(start, 2 * T), 2 * T)]
-
-    key_then = Fold(sends, recvs, 28).setup(key_quarter, None, land_k2, y_plus, y_minus)
-    value_then = Fold(sends, recvs, 34).setup(value_quarter, None, land_v2, z_plus, z_minus)
-    key_then.start()
-    value_then.start()
-    key_then.relay()
-    value_then.relay()
-    key_then.finish()
-    value_then.finish()
-
-    across = Lane(sends, recvs, 40)
-    block_k = pl.multiple_of((z * 4 + y) * RING * T, RING * T)
-    block_v = pl.multiple_of((y * 4 + z) * RING * T, RING * T)
+    for flip, step, _ in others:
+        hi = 1 - z_hi if flip else z_hi
+        origin = wrap(y - step)
+        spread.arrive(total.at[hi * RING + origin], flip * RING + step, ident(hi * 2 + z_lo, origin, x, c))
+    mine = c * KA + ka
+    near[mine] = jnp.sum(total[...], axis=0)
+    share = Lane(sends, recvs, 54)
+    for flip, step, peer in peers:
+        share.send(near.at[mine], near.at[mine], flip * KA + step, peer)
+
+    last_y.relay()
+    keys_z.relay(0)
+    values_y.relay()
+    keys_z.relay(1)
+    keys_z.finish(land_z.at[1])
+    last_y.finish()
+    keys_zy = Fold(sends, recvs, 34).setup(
+        lambda off, n: land_z.at[1, wrap(y + off), :, pl.ds(n * (T // 2), T // 2)], land_zy, y_plus, y_minus
+    )
+    keys_zy.start()
+    last_yz = Detour(sends, recvs, 44).setup(
+        lambda at: land_k.at[2 + lax.div(at, 2), pl.ds(lax.rem(at, 2), 1)], [pl.ds(0, 1)], land_kz, z, z_far, z_near
+    )
+    last_yz.start()
+    values_y.finish()
+    values_yz = Detour(sends, recvs, 40).setup(
+        lambda at: land_v.at[2 + lax.div(at, 2), lax.rem(at, 2)], [pl.ds(0, RING)], land_vz, z, z_far, z_near
+    )
+    values_yz.start()
+    keys_zy.relay()
+    last_yz.relay(0)
+    values_yz.relay(0)
+    lanes = pl.ds(pl.multiple_of(x * D, D), D)
+    key_factor, value_factor = key_gain[:, lanes], value_gain[:, lanes]
+    keys_zy.finish(key_factor)
+    for n in range(2):
+        final[0, 0 : RING - 1, n * (T // 2) : (n + 1) * (T // 2), :] = land_zy[2 + n]
+    last_yz.finish(final.at[0, pl.ds(RING - 1, 1)], key_factor)
+    values_yz.finish(final.at[1], value_factor)
+
+    across = Lane(sends, recvs, 48)
     for step in range(1, RING):
         to = wrap(x + step)
-        across.send(dk.at[pl.ds(block_k + to * T, T)], parts.at[0, x], step - 1, ident(z, y, to, c))
-        across.send(dv.at[pl.ds(block_v + to * T, T)], parts.at[1, x], step + 2, ident(z, y, to, c))
-    parts[0, x] = dk[pl.ds(block_k + x * T, T), :]
-    parts[1, x] = dv[pl.ds(block_v + x * T, T), :]
-    for step in range(1, RING):
-        origin = wrap(x - step)
-        across.arrive(parts.at[0, origin], step - 1, ident(z, y, origin, c))
-        across.arrive(parts.at[1, origin], step + 2, ident(z, y, origin, c))
-    for n in range(RING):
-        lanes = pl.ds(n * D, D)
-        dkey, dvalue = parts[0, n].astype(F32), parts[1, n].astype(F32)
-        grad_keys[:, lanes] = (dkey * key_gain[:, lanes]).astype(BF16)
-        grad_values[:, lanes] = (dvalue * value_gain[:, lanes]).astype(BF16)
-        sums[n : n + 1, :] = jnp.sum(dkey * keys[:, lanes].astype(F32), axis=0, keepdims=True)
-        sums[4 + n : 5 + n, :] = jnp.sum(dvalue * values[:, lanes].astype(F32), axis=0, keepdims=True)
-
-    mine = c * KA + ka
-    share = Lane(sends, recvs, 46)
-    for flip, step, peer in peers:
-        share.send(sums, near.at[mine], flip * KA + step, peer)
-    near[mine] = sums[...]
+        across.send(final.at[0, to], grad_keys.at[:, lanes], step - 1, ident(z, y, to, c))
+        across.send(final.at[1, to], grad_values.at[:, lanes], step + 2, ident(z, y, to, c))
+    grad_keys[:, lanes] = final[0, x]
+    grad_values[:, lanes] = final[1, x]
+
     for flip, step, _ in peers:
         origin = lax.rem(ka + KA - step, KA)
         core = 1 - c if flip else c
         from_ = ident(z_hi * 2 + lax.div(origin, 4), y, lax.rem(origin, 4), core)
         share.arrive(near.at[core * KA + origin], flip * KA + step, from_)
-    total[0] = jnp.sum(near[...], axis=0)
-    spread = Lane(sends, recvs, 62)
-    mine = z_hi * RING + y
-    for flip, step, other in others:
-        spread.send(total.at[0], total.at[1 + mine], flip * RING + step, other)
-    total[1 + mine] = total[0]
-    for flip, step, _ in others:
-        hi = 1 - z_hi if flip else z_hi
-        origin = wrap(y - step)
-        spread.arrive(total.at[1 + hi * RING + origin], flip * RING + step, ident(hi * 2 + z_lo, origin, x, c))
-    gains[...] = jnp.sum(total[1:], axis=0)
-
+    for n in range(RING):
+        whole = near[n] + near[RING + n] + near[2 * RING + n] + near[3 * RING + n]
+        grad_key_gain[:, n * D : (n + 1) * D] = whole[0:1]
+        grad_value_gain[:, n * D : (n + 1) * D] = whole[1:2]
+    for step in range(1, RING):
+        origin = wrap(x - step)
+        theirs = pl.ds(pl.multiple_of(origin * D, D), D)
+        across.arrive(grad_keys.at[:, theirs], step - 1, ident(z, y, origin, c))
+        across.arrive(grad_values.at[:, theirs], step + 2, ident(z, y, origin, c))
     for n in range(1, KA):
         origin = lax.rem(ka + KA - n, KA)
         their = head_columns(lax.div(origin, 4), lax.rem(origin, 4))
         from_ = ident(z_hi * 2 + lax.div(origin, 4), y, lax.rem(origin, 4), c)
         lane_q.arrive(grad_queries.at[:, their], n, from_)
-    for lane in [pair, lane_q, key_first, value_first, key_then, value_then, across, share, spread]:
+    for lane in [
+        pair, lane_q, keys_z, values_y, last_y, keys_zy, values_yz, last_yz, across, share, spread
+    ]:
         lane.drain()
 
 
 def shape(dims, dtype):
     return jax.ShapeDtypeStruct(dims, dtype)
+
+
+def attend_call(table, stats, queries, grad_out, sibling_rows, k, v, key_gain, value_gain):
+    vm, hbm = pl.BlockSpec(memory_space=pltpu.VMEM), pl.BlockSpec(memory_space=pl.ANY)
+    return pl.pallas_call(
+        attend,
+        out_shape=(shape((2 * KA * T, WIDTH), BF16), *[shape((RING, RING, RING, T, D), BF16)] * 2, shape((8, D), F32)),
+        in_specs=[pl.BlockSpec(memory_space=pltpu.SMEM)] + [hbm] * 6 + [vm] * 2,
+        out_specs=(vm,) * 4,
+        scratch_shapes=[
+            pltpu.SMEM((QUERY_TILES * KEY_TILES // 2 + 2,), jnp.int32),
+            pltpu.VMEM(stats.shape, F32),
+            pltpu.VMEM((2 * KA * T, WIDTH), BF16),
+            pltpu.VMEM((2 * KA * T, WIDTH), BF16),
+            pltpu.VMEM(k.shape, BF16),
+            pltpu.VMEM(v.shape, BF16),
+            pltpu.VMEM(k.shape, BF16),
+            pltpu.VMEM(v.shape, BF16),
+            pltpu.VMEM(k.shape, F32),
+            pltpu.VMEM(v.shape, F32),
+            pltpu.VMEM((QUERY_TILES, D, WIDTH), F32),
+            pltpu.VMEM((2, 2, 2 * T, WIDTH), BF16),
+            pltpu.VMEM((2, 8, D), F32),
+            pltpu.SemaphoreType.DMA((7,)),
+        ],
+        compiler_params=pltpu.CompilerParams(vmem_limit_bytes=47 * 2**20),
+        name="attend",
+    )(table, stats, queries, grad_out, sibling_rows, k, v, key_gain, value_gain)
 
 
 def shards(
@@ -582,90 +691,73 @@
     vm, hbm = pl.BlockSpec(memory_space=pltpu.VMEM), pl.BlockSpec(memory_space=pl.ANY)
     key_gain, value_gain = key_gain.reshape(1, -1), value_gain.reshape(1, -1)
     rows = queries.shape[0]
-    qg, gg, kg, vg, stats, table = pl.pallas_call(
+    sibling_rows, kg, vg, stats, table = pl.pallas_call(
         gather,
         out_shape=(
-            shape((2, rows, WIDTH), BF16),
             shape((2, rows, WIDTH), BF16),
             shape((RING, RING, RING * T, D), BF16),
             shape((RING, RING, RING * T, D), BF16),
             shape((QUERY_TILES, 2 * HEADS, T), F32),
             shape((QUERY_TILES, T), jnp.int32),
         ),
-        in_specs=[hbm, hbm] + [vm] * 9,
-        out_specs=(hbm, hbm, hbm, hbm, hbm, vm),
+        in_specs=[hbm] * 9,
+        out_specs=(hbm,) * 5,
         scratch_shapes=[
+            pltpu.VMEM((QUERY_TILES, T), jnp.int32),
             pltpu.VMEM(attn_out.shape, BF16),
-            pltpu.VMEM((RING, T, D), BF16),
-            pltpu.VMEM((RING, T, D), BF16),
+            pltpu.VMEM(log_sums.shape, F32),
+            pltpu.VMEM((1, T), jnp.int32),
+            pltpu.VMEM(tile_mask.shape, jnp.int32),
+            pltpu.VMEM((1, T), jnp.int32),
+            pltpu.VMEM(attn_out.shape, BF16),
             pltpu.VMEM((KA, 2 * HEADS, T), F32),
             pltpu.SemaphoreType.DMA((64,)),
             pltpu.SemaphoreType.DMA((64,)),
-            pltpu.SemaphoreType.DMA((6,)),
+            pltpu.SemaphoreType.DMA((12,)),
         ],
         compiler_params=pltpu.CompilerParams(
-            collective_id=0, has_side_effects=True, vmem_limit_bytes=32 * 2**20
+            collective_id=0, has_side_effects=True, vmem_limit_bytes=56 * 2**20
         ),
         name="gather",
     )(
-        queries, grad_out, key_rows, values, attn_out, log_sums, key_gain, value_gain,
+        queries, grad_out, key_rows, values, attn_out, log_sums,
         doc_ids.reshape(1, -1), tile_mask, block_order.reshape(1, -1),
     )
-    dq, dk, dv = pl.pallas_call(
-        attend,
-        out_shape=(
-            shape((2 * rows, WIDTH), BF16),
-            shape((KEY_TILES * T, D), BF16),
-            shape((KEY_TILES * T, D), BF16),
-        ),
-        in_specs=[pl.BlockSpec(memory_space=pltpu.SMEM)] + [vm] * 5,
-        out_specs=(vm, vm, vm),
-        scratch_shapes=[
-            pltpu.SMEM((QUERY_TILES * KEY_TILES // 2 + 2,), jnp.int32),
-            pltpu.VMEM((KEY_TILES * T, D), F32),
-            pltpu.VMEM((KEY_TILES * T, D), F32),
-            pltpu.VMEM((QUERY_TILES, D, WIDTH), F32),
-            pltpu.VMEM((2, 2, 2 * T, WIDTH), BF16),
-        ],
-        compiler_params=pltpu.CompilerParams(vmem_limit_bytes=56 * 2**20),
-        name="attend",
-    )(
-        table, stats, qg.reshape(2 * rows, WIDTH), gg.reshape(2 * rows, WIDTH),
-        kg.reshape(KEY_TILES * T, D), vg.reshape(KEY_TILES * T, D),
-    )
-    grad_queries, grad_keys, grad_values, gains = pl.pallas_call(
+    dq, dk, dv, partial = attend_call(
+        table, stats, queries, grad_out, sibling_rows,
+        kg.reshape(KEY_TILES * T, D), vg.reshape(KEY_TILES * T, D), key_gain, value_gain,
+    )
+    grad_queries, grad_keys, grad_values, grad_key_gain, grad_value_gain = pl.pallas_call(
         scatter,
         out_shape=(
             shape(attn_out.shape, BF16),
             shape(key_rows.shape, BF16),
             shape(values.shape, BF16),
-            shape((2 * RING, D), F32),
+            shape(key_gain.shape, F32),
+            shape(value_gain.shape, F32),
         ),
-        in_specs=[hbm] * 3 + [vm] * 4,
-        out_specs=(vm, vm, vm, vm),
+        in_specs=[vm] * 6,
+        out_specs=(vm,) * 5,
         scratch_shapes=[
-            pltpu.VMEM((KEY_TILES * T, D), BF16),
-            pltpu.VMEM((KEY_TILES * T, D), BF16),
-            pltpu.VMEM((rows, WIDTH), BF16),
-            pltpu.SemaphoreType.DMA((3,)),
             pltpu.VMEM((KA, T, WIDTH), BF16),
-            pltpu.VMEM((6, 2 * RING * T, D), BF16),
-            pltpu.VMEM((6, 2 * RING * T, D), BF16),
-            pltpu.VMEM((6, 2 * T, D), BF16),
-            pltpu.VMEM((6, 2 * T, D), BF16),
+            pltpu.VMEM((3, RING, RING - 1, T, D), BF16),
+            pltpu.VMEM((6, 2, RING, T, D), BF16),
+            pltpu.VMEM((6, 2, T, D), BF16),
+            pltpu.VMEM((6, RING - 1, T // 2, D), BF16),
+            pltpu.VMEM((3, RING, T, D), BF16),
+            pltpu.VMEM((3, 1, T, D), BF16),
             pltpu.VMEM((2, RING, T, D), BF16),
-            pltpu.VMEM((QUERY_TILES, 2 * RING, D), F32),
-            pltpu.VMEM((2 * RING, D), F32),
-            pltpu.VMEM((9, 2 * RING, D), F32),
-            pltpu.SemaphoreType.DMA((70,)),
-            pltpu.SemaphoreType.DMA((70,)),
+            pltpu.VMEM((QUERY_TILES, 8, D), F32),
+            pltpu.VMEM((8, 8, D), F32),
+            pltpu.SemaphoreType.DMA((78,)),
+            pltpu.SemaphoreType.DMA((78,)),
         ],
         compiler_params=pltpu.CompilerParams(
-            collective_id=1, has_side_effects=True, vmem_limit_bytes=48 * 2**20
+            collective_id=1, has_side_effects=True, vmem_limit_bytes=20 * 2**20
         ),
         name="scatter",
-    )(dq, dk, dv, key_rows, values, key_gain, value_gain)
-    return grad_queries, grad_keys, grad_values, gains[:RING].reshape(-1), gains[RING:].reshape(-1)
+    )(dq, dk, dv, partial, key_gain, value_gain)
+    return grad_queries, grad_keys, grad_values, grad_key_gain.reshape(-1), grad_value_gain.reshape(-1)
 
 
 def solution(mesh):

time: 177 us -> 137 us (0.77)
  Pallas kernels: 153 us -> 130 us
  local copies, waits for them, and re-layouts: 23.3 us -> 4.98 us
    unnamed x47 -> x13, local copies, waits for them, and re-layouts: 22.7 us -> 4.98 us
    pallas_call x2, Pallas kernels: 88.9 us -> 77.5 us  [the longest x1 41.1 us: attend_call(): pl.pallas_call(attend, out_shape=(shape((2 * KA * T, WIDTH), BF16), *[sha...]
    pallas_call x1, Pallas kernels: 64.1 us -> 52.8 us  [shards(): pl.pallas_call(scatter, out_shape=(shape(attn_out.shape, BF16), shape(key...]
where the time goes in v2:
time: 137 us; the launch traced here: 136 us
  Pallas kernels  130 us (95%)
  local copies, waits for them, and re-layouts  4.98 us (4%)
    pallas_call x1, Pallas kernels, shards(): pl.pallas_call(scatter, out_shape=(shape(attn_out.shape, BF16), shape(key...  52.8 us
    pallas_call x1, Pallas kernels, attend_call(): pl.pallas_call(attend, out_shape=(shape((2 * KA * T, WIDTH), BF16), *[sha...  41.1 us
    pallas_call x1, Pallas kernels, shards(): pl.pallas_call(gather, out_shape=(shape((2, rows, WIDTH), BF16), shape((R...  36.4 us
    unnamed x13, local copies, waits for them, and re-layouts  4.98 us

profile of v2, /device:TPU:1, one launch (start us, length us, event | category | flops | bytes accessed | tf_op | source)
XLA Modules:
  0.0 136.0 jit_solution(3578137538081945519)
XLA Ops:
  0.6 0.0 copy-start.2
  0.6 0.0 copy-start.3
  0.7 36.4 %gather.1 = (bf16[2,1024,512]{2,1,0:T(8,128)(2,1)}, bf16[4,4,512,128]{3,2,1,0:T(8,128)(2,1)}, bf16[4,4,512,128]{3,2,1,0:T(8,128)(2,1)}, f32[16,8,128]{2,1,0:T(8,128)}, s32[16,128]{1,0:T(8,128)}) custom-call(bf16[1024,4096]{1,0:T(8,128)(2,1)} %queries.3, bf16[1024,4096]{1,0:T(8,128)(2,1)} %grad_out.3, bf16[128,512]{1,0:T(8,128)(2,1)} %keys.1, ...), custom_call_target="tpu_custom_call" | custom-call | tf_op jit(solution)/shard_map/gather/pallas_call | solution.py:694
  37.1 0.0 copy-done.2
  37.1 0.0 copy-done.3
  37.1 0.0 copy-start
  37.1 0.8 copy-done
  37.9 0.0 copy-start.1
  37.9 0.7 copy-done.1
  38.6 41.1 %attend.1 = (bf16[2048,512]{1,0:T(8,128)(2,1)S(1)}, bf16[4,4,4,128,128]{4,3,2,1,0:T(8,128)(2,1)S(1)}, bf16[4,4,4,128,128]{4,3,2,1,0:T(8,128)(2,1)S(1)}, f32[8,128]{1,0:T(8,128)S(1)}) custom-call(s32[16,128]{1,0:T(8,128)S(1)} %copy-done.1, f32[16,8,128]{2,1,0:T(8,128)S(1)} %copy-done, bf16[1024,4096]{1,0:T(8,128)(2,1)} %queries.3, ...), custom_call_target="tpu_custom_call" | custom-call | tf_op jit(solution)/shard_map/attend/pallas_call | solution.py:662
  79.8 52.8 %scatter.1 = (bf16[128,4096]{1,0:T(8,128)(2,1)S(1)}, bf16[128,512]{1,0:T(8,128)(2,1)S(1)}, bf16[128,512]{1,0:T(8,128)(2,1)S(1)}, f32[1,512]{1,0:T(1,128)S(1)}, f32[1,512]{1,0:T(1,128)S(1)}) custom-call(bf16[2048,512]{1,0:T(8,128)(2,1)S(1)} %get-tuple-element.24.dq, bf16[4,4,4,128,128]{4,3,2,1,0:T(8,128)(2,1)S(1)} %get-tuple-element.25.dk, ...), custom_call_target="tpu_custom_call" | custom-call | tf_op jit(solution)/shard_map/scatter/pallas_call | solution.py:730
  132.6 1.0 copy.21
  133.6 0.7 copy.22
  134.2 0.7 copy.23
  134.9 0.6 copy.24
  135.5 0.6 copy.25
Async XLA Ops:
  0.6 36.4 %copy-start.2 = (f32[512]{0:T(512)S(1)}, f32[512]{0:T(512)}, u32[]{:S(2)}) copy-start(f32[512]{0:T(512)} %param.17) | copy-start | bytes 6148
  0.6 36.4 %copy-start.3 = (f32[512]{0:T(512)S(1)}, f32[512]{0:T(512)}, u32[]{:S(2)}) copy-start(f32[512]{0:T(512)} %param.18) | copy-start | bytes 6148
  37.1 0.8 copy-start
  37.9 0.7 copy-start.1
